TPU v7x, 32 devices: a whole 2x2x4 slice. The times are simulated.
32 devices in a mesh: sta: 16 (over z, y, core), band: 2 (over x).
Axes of the slice: x: 2, y: 2, z: 4, core: 2. Of those that a mesh axis runs over, the one named last changes fastest.
Arguments:
- spectra: bfloat16 [256, 2, 2, 4096], P('sta', None, None, 'band')
- flags: int32 [256, 2], P('sta'), may hold values 0 or 1
- passband: int32 [256, 2], P('sta'), may hold values from 0 to 4096, as said below
Outputs:
- correlation: float32 [256, 32, 256], P('sta', None, 'band')
Inputs may be any that keep to these rules, and one draw needn't show every extreme that they name: 0 <= passband[s, 0] < 512 and 3584 < passband[s, 1]; some station starts at 0 and some ends at 4096.
All inputs are finite; a program needn't handle non-finite values. No bound on the sum of `flags` on one device may be relied on, other than what follows from the above.
Results may differ from a plain program's by a relative error of at most 0.0044.
Values may be sent and summed in bfloat16 or wider, within the bound.
A program may use at most 64 MiB of HBM per device.

v0:
```python
import math

import jax
import jax.numpy as jnp
from jax import lax
from jax.sharding import PartitionSpec as P

SEG = 2
FREQ = 4096
LAGS = 32


def passband_mask(passband, freq_index):
    lower_ok = freq_index[None, :] >= passband[:, 0:1]
    upper_ok = freq_index[None, :] < passband[:, 1:2]
    return (lower_ok & upper_ok).astype(jnp.float32)


def lag_tables(freq_index):
    lag_index = jnp.arange(LAGS, dtype=jnp.int32) - LAGS // 2
    turns = jnp.mod(lag_index[:, None] * freq_index[None, :], FREQ)
    phases = turns.astype(jnp.float32) * (2.0 * math.pi / FREQ)
    return (jnp.cos(phases), jnp.sin(phases))


def rotate(whitened, cosine, sine_table):
    real_part = whitened[:, :, 0, :].astype(jnp.float32)[:, None]
    imag_part = whitened[:, :, 1, :].astype(jnp.float32)[:, None]
    cos_b = cosine[None, :, None, :]
    sin_b = sine_table[None, :, None, :]
    rot_real = real_part * cos_b - imag_part * sin_b
    rot_imag = imag_part * cos_b + real_part * sin_b
    return jnp.stack([rot_real, rot_imag], axis=3).astype(jnp.bfloat16)


def local(spectra, flags, passband):
    local_rows = spectra.shape[0]
    local_freq = spectra.shape[3]
    band_index = lax.axis_index("band")
    band_count = lax.axis_size("band")
    all_stations = local_rows * lax.axis_size("sta")
    share_cols = all_stations // band_count
    freq_index = band_index * local_freq + jnp.arange(local_freq, dtype=jnp.int32)
    kept = passband_mask(passband, freq_index)
    values = spectra.astype(jnp.float32)
    partial_energy = jnp.sum(values * values * kept[:, None, None, :], axis=(2, 3))
    energy = lax.psum(partial_energy, "band")
    band_width = (passband[:, 1] - passband[:, 0]).astype(jnp.float32)
    root_mean = jnp.sqrt(energy / band_width[:, None] + 1e-06)
    valid = flags.astype(jnp.float32)
    whitened = (
        values * (kept[:, None, None, :] * valid[:, :, None, None] / root_mean[:, :, None, None])
    ).astype(jnp.bfloat16)
    cosine, sine_table = lag_tables(freq_index)
    inner = SEG * 2 * local_freq
    rotated = rotate(whitened, cosine, sine_table).reshape(local_rows * LAGS, inner)
    flat_rows = whitened.reshape(local_rows, inner)
    shard_rows = lax.all_gather(flat_rows, "sta", axis=0, tiled=True)
    product = lax.dot_general(
        rotated, shard_rows, (((1,), (1,)), ((), ())), preferred_element_type=jnp.float32
    )
    product = product.reshape(local_rows, LAGS, shard_rows.shape[0])
    flag_rows = lax.all_gather(flags, "sta", axis=0, tiled=True)
    pairs = jnp.dot(valid, flag_rows.astype(jnp.float32).T, preferred_element_type=jnp.float32)
    summed = lax.psum_scatter(product, "band", scatter_dimension=2, tiled=True)
    pair_share = lax.dynamic_slice_in_dim(pairs, band_index * share_cols, share_cols, 1)
    return summed / (jnp.maximum(pair_share, 1.0)[:, None, :] * math.sqrt(FREQ))


def solution(mesh):
    placed = (P("sta", None, None, "band"), P("sta", None), P("sta", None))
    return jax.shard_map(
        local, mesh=mesh, in_specs=placed, out_specs=P("sta", None, "band"), check_vma=False
    )
```

profile of v0, /device:TPU:0, one launch (start us, length us, event | category | flops | bytes accessed | tf_op | source)
XLA Modules:
  0.0 110.5 jit_solution(18001790350000959470)
XLA Ops:
  6.5 0.0 all-gather.3.cloned.1.call-start
  6.5 0.8 convert_bitcast_fusion
  7.3 0.1 and_convert_fusion
  7.4 1.2 %fusion.3 = f32[16,2]{0,1:T(2,128)S(1)} fusion(f32[16,2048]{1,0:T(8,128)S(1)} %and_convert_fusion, bf16[16,2,2,2048]{3,2,1,0:T(2,128)(2,1)} %param.3), kind=kLoop, calls=%fused_computation.8 | loop fusion | flops 524256 | bytes 393344 | tf_op jit(solution)/shard_map/reduce_sum | solution.py:46
  8.6 5.8 %psum.7 = f32[16,2]{0,1:T(2,128)S(1)} all-reduce(f32[16,2]{0,1:T(2,128)S(1)} %fusion.3), channel_id=1, replica_groups=mesh['sta'=16,'band'=2] {'band'}, use_global_device_ids=true, to_apply=%region_1.0 | all-reduce | flops 32 | bytes 256 | tf_op jit(solution)/shard_map/psum | solution.py:47
  14.4 0.7 convert_element_type.60
  15.1 0.1 multiply_divide_fusion
  15.2 1.1 %fusion.4 = bf16[16,2,2,2048]{3,0,2,1:T(8,128)(2,1)S(1)} fusion(f32[16,2,2048]{2,0,1:T(8,128)S(1)} %multiply_divide_fusion, bf16[16,2,2,2048]{3,2,1,0:T(2,128)(2,1)} %param.3), kind=kLoop, calls=%fused_computation.9 | loop fusion | flops 393216 | bytes 786432 | tf_op jit(solution)/shard_map/convert_element_type | solution.py:53
  16.3 0.3 copy.18
  16.6 0.9 reshape.157
  17.5 0.0 all-gather.3.cloned.1.call-update
  17.5 0.0 reduce-scatter.2.cloned.1.call-start
  17.6 0.2 copy.16
  17.8 0.2 copy.17
  18.0 1.1 fusion.11
  19.1 17.8 %subtract_convert_fusion = (bf16[16,32,2,1,2048]{4,3,2,1,0:T(2,128)(2,1)S(1)}, bf16[16,32,2,1,2048]{4,3,2,1,0:T(2,128)(2,1)S(1)}) fusion(f32[32,2048]{1,0:T(8,128)S(1)} %get-tuple-element.10, f32[16,2,2048]{2,1,0:T(2,128)S(1)} %copy.17, f32[32,2048]{1,0:T(8,128)S(1)} %get-tuple-element.9, f32[16,2,2048]{2,1,0:T(2,128)S(1)} %copy.16), kind=kLoop, calls=%fused_computation.2 | loop fusion | flops 16777216 | bytes 9437184 | tf_op jit(solution)/shard_map/convert.2
  36.9 20.3 %pad_maximum_fusion = bf16[16,32,2,2,2048]{4,3,2,1,0:T(2,128)(2,1)} fusion(bf16[16,32,2,1,2048]{4,3,2,1,0:T(2,128)(2,1)S(1)} %get-tuple-element.6, bf16[16,32,2,1,2048]{4,3,2,1,0:T(2,128)(2,1)S(1)} %get-tuple-element.5), kind=kLoop, calls=%fused_computation | loop fusion | flops 16777216 | bytes 16777216 | tf_op jit(solution)/shard_map/stack | solution.py:33
  57.2 14.6 %convert_element_type.68 = bf16[16,32,8192]{2,1,0:T(8,128)(2,1)} reshape(bf16[16,32,2,2,2048]{4,3,2,1,0:T(2,128)(2,1)} %pad_maximum_fusion) | data formatting | bytes 16777216 | tf_op jit(solution)/shard_map/convert_element_type | solution.py:33
  71.8 0.0 copy-start
  71.8 0.0 all-gather.3.cloned.1.call-done
  71.8 7.8 %fusion = f32[16,32,256]{2,1,0:T(8,128)} fusion(bf16[16,32,8192]{2,1,0:T(8,128)(2,1)} %convert_element_type.68, bf16[256,8192]{1,0:T(8,128)(2,1)} %all-gather.3.cloned.1.call-done), kind=kOutput, calls=%fused_computation.3 | convolution fusion | flops 2147483648 | bytes 13107200 | tf_op jit(solution)/shard_map/dot_general | solution.py:59
  79.6 0.0 reduce-scatter.2.cloned.1.call-update
  79.6 0.0 copy-done
  79.6 22.1 %all-gather = s32[16,16,2]{1,2,0:T(2,128)S(1)} all-gather(s32[1,16,2]{1,2,0:T(2,128)S(1)} %bitcast.24), channel_id=1, replica_groups=mesh['sta'=16,'band'=2] {'sta'}, dimensions={0}, use_global_device_ids=true | all-gather | bytes 2176 | tf_op jit(solution)/shard_map/all_gather | solution.py:63
  101.7 0.1 reshape.162
  101.8 0.2 fusion.12
  102.0 0.0 reduce-scatter.2.cloned.1.call-done
  102.0 1.7 %broadcast_divide_fusion = f32[16,32,128]{2,1,0:T(8,128)} fusion(f32[16,32,128]{2,1,0:T(8,128)} %reduce-scatter.2.cloned.1.call-done, f32[16,128]{1,0:T(8,128)S(1)} %maximum_multiply_fusion), kind=kLoop, calls=%fused_computation.23 | loop fusion | flops 65536 | bytes 532480 | tf_op jit(solution)/shard_map/div | solution.py:67
  (6 shorter events, 0.1 us)
Async XLA Ops:
  6.5 65.3 %all-gather.3.cloned.1.call-start = ((), (), s32[]{:S(2)}) async-start(), calls=%async_computation.1 | async-start | bytes 4456448 | tf_op jit(solution)/shard_map/all_gather | solution.py:58
  17.5 84.5 %reduce-scatter.2.cloned.1.call-start = ((), (), s32[]{:S(2)}) async-start(), calls=%async_computation.2 | async-start | bytes 786432 | tf_op jit(solution)/shard_map/reduce_scatter | solution.py:65
  71.8 7.8 %copy-start = (s32[16,2]{0,1:T(2,128)S(1)}, s32[16,2]{0,1:T(2,128)}, u32[]{:S(2)}) copy-start(s32[16,2]{0,1:T(2,128)} %param.4) | copy-start | bytes 388
Sparse Core Ops, SparseCore 0:
  17.6 52.3 all-gather.2
  79.7 16.2 reduce-scatter.1
where the time goes:
time: 111 us
  other arithmetic  44.9 us (40%)
  blocking collectives  27.9 us (25%)
  local copies, waits for them, and re-layouts  16.2 us (15%)
  between operations  13.5 us (12%)
  matrix products  7.98 us (7%)
    all_gather x1, blocking collectives, local(): flag_rows = lax.all_gather(flags, 'sta', axis=0, tiled=True)  22.1 us
    another operation x1, other arithmetic, rotate(): return jnp.stack([rot_real, rot_imag], axis=3).astype(jnp.bfloat16)  20.3 us
    another operation x1, other arithmetic  17.8 us
    convert_element_type x1, local copies, waits for them, and re-layouts, rotate(): return jnp.stack([rot_real, rot_imag], axis=3).astype(jnp.bfloat16)  14.6 us
    dot_general x1, matrix products, local(): lax.dot_general(rotated, shard_rows, (((1,), (1,)), ((), ())), preferred_...  7.79 us
    psum x1, blocking collectives, local(): energy = lax.psum(partial_energy, 'band')  5.82 us
  transfers between devices with their start and end apart: 2, of which 0 were waited for; matrix products, arithmetic and copies ran while one was open for 49% of the time, Pallas kernels for 0%

commit v1 on v0

v1 whole, which is shorter than its diff:
```python
import functools
import math

import jax
import jax.numpy as jnp
from jax import lax
from jax.experimental import pallas as pl
from jax.experimental.pallas import tpu as pltpu
from jax.sharding import PartitionSpec as P

FREQ = 4096
LAGS = 32
SEG = 2
PIECES = 4
EXT = 128
MESH = pl.DeviceIdType.MESH


def station_of(position, core, chips):
    half = chips // 2
    if chips == 8:
        chip = jnp.where(position < half, 2 * position, 2 * (chips - 1 - position) + 1)
    else:
        chip = jnp.where(position < half, position, half + (chips - 1 - position))
    return 2 * chip + core


def position_of(chip, chips):
    half = chips // 2
    if chips == 8:
        return jnp.where(chip % 2 == 0, chip // 2, chips - 1 - chip // 2)
    return jnp.where(chip < half, chip, chips - 1 - (chip - half))


def kernel(
    n, nb, x_ref, flags_ref, band_ref, out_ref,
    w, rot, cos_ref, sin_ref, acc, energies, part, got,
    ring_send, ring_recv, sib_send, sib_recv, en_send, en_recv, part_send, part_recv,
):
    rows, wide = x_ref.shape
    freq = wide // (2 * SEG)
    half = freq // 2
    depth = 2 * half
    chips = n // 2
    share = n * rows // nb
    me = lax.axis_index("sta")
    band = lax.axis_index("band")
    core = lax.rem(me, 2)
    pos = position_of(me // 2, chips)
    sibling = me + 1 - 2 * core

    def at_pos(offset, own_core):
        return station_of(lax.rem(pos + offset + chips, chips), own_core, chips)

    right, left = at_pos(1, core), at_pos(-1, core)

    barrier = pltpu.get_barrier_semaphore()
    for other in (right, left, sibling):
        pl.semaphore_signal(barrier, inc=1, device_id={"sta": other}, device_id_type=MESH)
    for k in range(1, nb):
        pl.semaphore_signal(
            barrier, inc=1, device_id={"band": lax.rem(band + k, nb)}, device_id_type=MESH
        )

    f_index = band * freq + lax.broadcasted_iota(jnp.int32, (rows, freq), 1)
    kept = (f_index >= band_ref[:, 0:1]) & (f_index < band_ref[:, 1:2])
    lane = lax.broadcasted_iota(jnp.int32, (rows, EXT), 1)
    sums, undo = [], []
    for g in range(SEG):
        vals = []
        for c in range(2):
            start = (g * 2 + c) * freq
            v = x_ref[:, start:start + freq].astype(jnp.float32)
            vals.append(jnp.where(kept, v, 0.0))
        e = jnp.sum(vals[0] * vals[0] + vals[1] * vals[1], axis=1, keepdims=True)
        big = jnp.where(e < 3.0e38, 2.0 ** -40, 0.0)
        fac = jnp.where(e < 2.0 ** -60, 2.0 ** 40, jnp.where(e > 2.0 ** 80, big, 1.0))
        undo.append(jnp.where(e < 2.0 ** -60, 2.0 ** -40, jnp.where(e > 2.0 ** 80, 2.0 ** 40, 1.0)))
        sums.append(e)
        for h in range(2):
            for c in range(2):
                w[2 * g + h, me, :, c * half:(c + 1) * half] = (
                    vals[c][:, h * half:(h + 1) * half] * fac
                ).astype(jnp.bfloat16)
    energies[band] = jnp.where(lane == 0, sums[0], jnp.where(lane == 1, sums[1], 0.0))

    pl.semaphore_wait(barrier, 3 + nb - 1)

    en_copies = []
    for k in range(1, nb):
        en_copies.append(pltpu.make_async_remote_copy(
            src_ref=energies.at[band], dst_ref=energies.at[band],
            send_sem=en_send.at[k], recv_sem=en_recv.at[k],
            device_id={"band": lax.rem(band + k, nb)}, device_id_type=MESH,
        ))
        en_copies[-1].start()

    def view(p, s):
        return w.at[p, s] if p == PIECES - 1 else w.at[p, s, :, 0:depth]

    def ring(p, way, t, s):
        return pltpu.make_async_remote_copy(
            src_ref=view(p, s), dst_ref=view(p, s),
            send_sem=ring_send.at[way, p, t], recv_sem=ring_recv.at[way, p, t],
            device_id={"sta": right if way == 0 else left}, device_id_type=MESH,
        )

    def across(p, k, s):
        return pltpu.make_async_remote_copy(
            src_ref=view(p, s), dst_ref=view(p, s),
            send_sem=sib_send.at[p, k], recv_sem=sib_recv.at[p, k],
            device_id={"sta": sibling}, device_id_type=MESH,
        )

    long = chips // 2
    hops = [(long, chips - 1 - long) if p % 2 == 0 else (chips - 1 - long, long)
            for p in range(PIECES)]
    sent = []

    def go(copy):
        copy.start()
        sent.append(copy)

    def send_own(p):
        for way in range(2):
            if hops[p][way] > 0:
                go(ring(p, way, 0, me))
        go(across(p, 0, me))

    for p in range(PIECES - 1):
        send_own(p)

    for k in range(1, nb):
        source = lax.rem(band + nb - k, nb)
        pltpu.make_async_remote_copy(
            src_ref=energies.at[source], dst_ref=energies.at[source],
            send_sem=en_send.at[k], recv_sem=en_recv.at[k],
            device_id={"band": source}, device_id_type=MESH,
        ).wait_recv()
    total = energies[0]
    for k in range(1, nb):
        total = total + energies[k]
    width = (band_ref[:, 1:2] - band_ref[:, 0:1]).astype(jnp.float32)
    ext = jnp.zeros((rows, EXT), jnp.float32)
    own = []
    for g in range(SEG):
        valid = flags_ref[:, g:g + 1].astype(jnp.float32)
        factor = valid / jnp.sqrt(total[:, g:g + 1] / width + 1e-06) * undo[g]
        own.append(factor)
        rest = factor
        for i in range(3):
            term = rest.astype(jnp.bfloat16).astype(jnp.float32)
            rest = rest - term
            ext = jnp.where(lane == 3 * g + i, term, ext)
        ext = jnp.where(lane == 6 + g, valid, ext)
    w[PIECES - 1, me, :, depth:depth + EXT] = ext.astype(jnp.bfloat16)
    send_own(PIECES - 1)

    @pl.loop(0, freq // 128)
    def _(j):
        cols = pl.ds(pl.multiple_of(j * 128, 128), 128)
        lag = lax.broadcasted_iota(jnp.int32, (LAGS, 128), 0) - LAGS // 2
        f = band * freq + j * 128 + lax.broadcasted_iota(jnp.int32, (LAGS, 128), 1)
        turns = ((lag * f + FREQ // 2) & (FREQ - 1)) - FREQ // 2
        phase = turns.astype(jnp.float32) * (2.0 * math.pi / FREQ)
        cos_ref[:, cols] = jnp.cos(phase)
        sin_ref[:, cols] = jnp.sin(phase)

    def rotate(p):
        h = p % 2

        @pl.loop(0, half // 128)
        def _(j):
            at = pl.multiple_of(j * 128, 128)
            table = pl.ds(pl.multiple_of(h * half + j * 128, 128), 128)
            cosine, sine = cos_ref[:, table], sin_ref[:, table]
            re = w[p, me, :, pl.ds(at, 128)].astype(jnp.float32)
            im = w[p, me, :, pl.ds(pl.multiple_of(half + j * 128, 128), 128)].astype(jnp.float32)
            for a in range(rows):
                r, i = re[a:a + 1], im[a:a + 1]
                lines = slice(a * LAGS, (a + 1) * LAGS)
                rot[p, lines, pl.ds(at, 128)] = (r * cosine - i * sine).astype(jnp.bfloat16)
                rot[p, lines, pl.ds(pl.multiple_of(half + j * 128, 128), 128)] = (
                    i * cosine + r * sine
                ).astype(jnp.bfloat16)

    def hop(p, t):
        for way in range(2):
            if t <= hops[p][way]:
                s = at_pos(-t if way == 0 else t, core)
                ring(p, way, t - 1, s).wait_recv()
                if t < hops[p][way]:
                    go(ring(p, way, t, s))
                go(across(p, t if way == 0 else hops[p][0] + t, s))

    def multiply(p):
        g = p // 2
        for k in range(chips):
            t = k if k <= hops[p][0] else k - hops[p][0]
            s = at_pos(-t if k <= hops[p][0] else t, 1 - core)
            across(p, k, s).wait_recv()
        step = min(depth, 512)

        @pl.loop(0, depth // step)
        def _(j):
            cols = pl.ds(pl.multiple_of(j * step, step), step)
            term = lax.dot_general(
                rot[p, :, cols], w[p, :, :, cols].reshape(n * rows, step),
                (((1,), (1,)), ((), ())), preferred_element_type=jnp.float32,
            )
            if p % 2 == 0:
                @pl.when(j == 0)
                def _():
                    acc[g] = term

                @pl.when(j > 0)
                def _():
                    acc[g] += term
            else:
                acc[g] += term

    for t in range(1, long + 1):
        for p in range(PIECES):
            hop(p, t)
            if t == 1:
                rotate(p)
            if t == long:
                multiply(p)

    ext_all = w[PIECES - 1, :, :, depth:depth + EXT].reshape(n * rows, EXT)
    row = lax.broadcasted_iota(jnp.int32, (16, EXT), 0)
    col = lax.broadcasted_iota(jnp.int32, (16, EXT), 1)
    pick = ((row < SEG) & (col >= 3 * row) & (col < 3 * row + 3)).astype(jnp.float32)
    nt = (((1,), (1,)), ((), ()))
    theirs = lax.dot_general(
        pick.astype(jnp.bfloat16), ext_all, nt, preferred_element_type=jnp.float32
    )
    flag_cols = jnp.where((lane >= 6) & (lane < 6 + SEG), ext, 0.0).astype(jnp.bfloat16)
    pairs = lax.dot_general(flag_cols, ext_all, nt, preferred_element_type=jnp.float32)
    denominator = 1.0 / (jnp.maximum(pairs, 1.0) * math.sqrt(FREQ))
    weight = [own[g] * theirs[g:g + 1] * denominator for g in range(SEG)]

    for q in range(nb):
        cols = slice(q * share, (q + 1) * share)
        for a in range(rows):
            lines = slice(a * LAGS, (a + 1) * LAGS)
            part[q, lines] = (
                acc[0, lines, cols] * weight[0][a:a + 1, cols]
                + acc[1, lines, cols] * weight[1][a:a + 1, cols]
            )
    copies = []
    for k in range(1, nb):
        target = lax.rem(band + k, nb)
        copies.append(pltpu.make_async_remote_copy(
            src_ref=part.at[target], dst_ref=got.at[k],
            send_sem=part_send.at[k], recv_sem=part_recv.at[k],
            device_id={"band": target}, device_id_type=MESH,
        ))
        copies[-1].start()
    for copy in sent + en_copies:
        copy.wait_send()
    for copy in copies:
        copy.wait()
    result = part[band]
    for k in range(1, nb):
        result = result + got[k]
    out_ref[...] = result


def solution(mesh):
    n, nb = mesh.shape["sta"], mesh.shape["band"]

    def local(spectra, flags, passband):
        rows, _, _, freq = spectra.shape
        share = n * rows // nb
        depth = freq
        vmem = pl.BlockSpec(memory_space=pltpu.VMEM)
        chips = n // 2
        dma = pltpu.SemaphoreType.DMA
        out = pl.pallas_call(
            functools.partial(kernel, n, nb),
            out_shape=jax.ShapeDtypeStruct((rows * LAGS, share), jnp.float32),
            in_specs=[vmem] * 3,
            out_specs=vmem,
            scratch_shapes=[
                pltpu.VMEM((PIECES, n, rows, depth + EXT), jnp.bfloat16),
                pltpu.VMEM((PIECES, rows * LAGS, depth), jnp.bfloat16),
                pltpu.VMEM((LAGS, freq), jnp.float32),
                pltpu.VMEM((LAGS, freq), jnp.float32),
                pltpu.VMEM((SEG, rows * LAGS, n * rows), jnp.float32),
                pltpu.VMEM((nb, rows, EXT), jnp.float32),
                pltpu.VMEM((nb, rows * LAGS, share), jnp.float32),
                pltpu.VMEM((nb, rows * LAGS, share), jnp.float32),
                dma((2, PIECES, chips)), dma((2, PIECES, chips)),
                dma((PIECES, chips)), dma((PIECES, chips)),
                dma((nb,)), dma((nb,)), dma((nb,)), dma((nb,)),
            ],
            compiler_params=pltpu.CompilerParams(
                collective_id=0, has_side_effects=True, vmem_limit_bytes=48 * 1024 * 1024
            ),
        )(spectra.reshape(rows, SEG * 2 * freq), flags, passband)
        return out.reshape(rows, LAGS, share)

    placed = (P("sta", None, None, "band"), P("sta", None), P("sta", None))
    return jax.shard_map(
        local, mesh=mesh, in_specs=placed, out_specs=P("sta", None, "band"), check_vma=False
    )
```

time: 111 us -> 46 us (0.41)
  other arithmetic: 44.9 us -> 0 us
  Pallas kernels: 0 us -> 43.2 us
  blocking collectives: 27.9 us -> 0 us
  local copies, waits for them, and re-layouts: 16.2 us -> 2.69 us
  between operations: 13.5 us -> 0.01 us
  matrix products: 7.98 us -> 0 us
    pallas_call x0 -> x1, Pallas kernels: none -> 43.2 us  [local(): pl.pallas_call(functools.partial(kernel, n, nb), out_shape=jax.ShapeDtype...]
    another operation x2 -> x0, other arithmetic: 38.1 us -> none  [the longest x1 20.3 us: rotate(): return jnp.stack([rot_real, rot_imag], axis=3).astype(jnp.bfloat16)]
    all_gather x1 -> x0, blocking collectives: 22.1 us -> none  [local(): flag_rows = lax.all_gather(flags, 'sta', axis=0, tiled=True)]
    convert_element_type x5 -> x0, local copies, waits for them, and re-layouts: 15.3 us -> none  [the longest x1 14.6 us: rotate(): return jnp.stack([rot_real, rot_imag], axis=3).astype(jnp.bfloat16)]
    dot_general x2 -> x0, matrix products: 7.98 us -> none  [the longest x1 7.79 us: local(): lax.dot_general(rotated, shard_rows, (((1,), (1,)), ((), ())), preferred_...]
    psum x1 -> x0, blocking collectives: 5.82 us -> none  [local(): energy = lax.psum(partial_energy, 'band')]
    div x3 -> x0, other arithmetic: 2.54 us -> none  [the longest x1 1.68 us: local(): return summed / (jnp.maximum(pair_share, 1.0)[:, None, :] * math.sqrt(FREQ))]
    convert_element_type x5 -> x0, other arithmetic: 1.93 us -> none  [the longest x1 1.12 us: local(): whitened = (values * (kept[:, None, None, :] * valid[:, :, None, None] /...]
  transfers between devices with their start and end apart: 2 -> 0, of which waited for: 0 -> 0; matrix products, arithmetic and copies ran while one was open for 49% -> 0% of each run, Pallas kernels for 0% -> 0%
where the time goes in v1:
time: 46 us; the launch traced here: 45.9 us
  Pallas kernels  43.2 us (94%)
  local copies, waits for them, and re-layouts  2.69 us (6%)
    pallas_call x1, Pallas kernels, local(): pl.pallas_call(functools.partial(kernel, n, nb), out_shape=jax.ShapeDtype...  43.2 us
    unnamed x5, local copies, waits for them, and re-layouts  1.56 us
    reshape x1, local copies, waits for them, and re-layouts, local(): spectra.reshape(rows, SEG * 2 * freq)  1.13 us

profile of v1, /device:TPU:0, one launch (start us, length us, event | category | flops | bytes accessed | tf_op | source)
XLA Modules:
  0.0 45.9 jit_solution(18022137095560712149)
XLA Ops:
  0.0 0.0 copy-start
  0.0 0.8 %copy.4.flags_ref = s32[16,2]{1,0:T(8,128)S(1)} copy(s32[16,2]{0,1:T(2,128)} %param.4) | data formatting | bytes 256 | tf_op args[1]
  0.8 0.0 copy-done
  0.8 0.1 copy.5.band_ref
  0.9 1.1 %reshape.6.x_ref = bf16[16,8192]{1,0:T(8,128)(2,1)S(1)} reshape(bf16[16,2,2,2048]{3,2,1,0:T(2,128)(2,1)} %param.3) | data formatting | bytes 524288 | tf_op jit(solution)/shard_map/reshape | solution.py:301
  2.0 43.2 %shard_map.37 = f32[512,128]{1,0:T(8,128)S(1)} custom-call(bf16[16,8192]{1,0:T(8,128)(2,1)S(1)} %reshape.6.x_ref, s32[16,2]{1,0:T(8,128)S(1)} %copy.4.flags_ref, s32[16,2]{1,0:T(8,128)S(1)} %copy.5.band_ref), custom_call_target="tpu_custom_call" | custom-call | tf_op jit(solution)/shard_map/pallas_call | solution.py:280
  45.2 0.7 %copy.7 = f32[16,32,128]{2,1,0:T(8,128)} copy(f32[16,32,128]{2,1,0:T(8,128)S(1)} %bitcast.1) | data formatting | bytes 524288
Async XLA Ops:
  0.0 0.8 %copy-start = (s32[16,2]{0,1:T(2,128)S(1)}, s32[16,2]{0,1:T(2,128)}, u32[]{:S(2)}) copy-start(s32[16,2]{0,1:T(2,128)} %param.5) | copy-start | bytes 388

commit v2 on v1

--- a/solution.py
+++ b/solution.py
@@ -34,7 +34,7 @@
 
 def kernel(
     n, nb, x_ref, flags_ref, band_ref, out_ref,
-    w, rot, cos_ref, sin_ref, acc, energies, part, got,
+    w, rot, cos_ref, sin_ref, acc, energies, weight, part, got,
     ring_send, ring_recv, sib_send, sib_recv, en_send, en_recv, part_send, part_recv,
 ):
     rows, wide = x_ref.shape
@@ -127,8 +127,8 @@
                 go(ring(p, way, 0, me))
         go(across(p, 0, me))
 
-    for p in range(PIECES - 1):
-        send_own(p)
+    send_own(0)
+    send_own(1)
 
     for k in range(1, nb):
         source = lax.rem(band + nb - k, nb)
@@ -154,7 +154,6 @@
             ext = jnp.where(lane == 3 * g + i, term, ext)
         ext = jnp.where(lane == 6 + g, valid, ext)
     w[PIECES - 1, me, :, depth:depth + EXT] = ext.astype(jnp.bfloat16)
-    send_own(PIECES - 1)
 
     @pl.loop(0, freq // 128)
     def _(j):
@@ -193,39 +192,50 @@
                     go(ring(p, way, t, s))
                 go(across(p, t if way == 0 else hops[p][0] + t, s))
 
-    def multiply(p):
-        g = p // 2
+    def gathered(p):
         for k in range(chips):
             t = k if k <= hops[p][0] else k - hops[p][0]
             s = at_pos(-t if k <= hops[p][0] else t, 1 - core)
             across(p, k, s).wait_recv()
+
+    def multiply(p, lines):
+        g = p // 2
         step = min(depth, 512)
 
         @pl.loop(0, depth // step)
         def _(j):
             cols = pl.ds(pl.multiple_of(j * step, step), step)
             term = lax.dot_general(
-                rot[p, :, cols], w[p, :, :, cols].reshape(n * rows, step),
+                rot[p, lines, cols], w[p, :, :, cols].reshape(n * rows, step),
                 (((1,), (1,)), ((), ())), preferred_element_type=jnp.float32,
             )
             if p % 2 == 0:
                 @pl.when(j == 0)
                 def _():
-                    acc[g] = term
+                    acc[g, lines] = term
 
                 @pl.when(j > 0)
                 def _():
-                    acc[g] += term
+                    acc[g, lines] += term
             else:
-                acc[g] += term
-
-    for t in range(1, long + 1):
-        for p in range(PIECES):
-            hop(p, t)
-            if t == 1:
-                rotate(p)
-            if t == long:
-                multiply(p)
+                acc[g, lines] += term
+
+    order = sorted(
+        ((p, t) for p in range(PIECES) for t in range(1, long + 1)),
+        key=lambda pt: (pt[0] + pt[1], -pt[0]),
+    )
+    rotated = 0
+    for p, t in order:
+        hop(p, t)
+        if p == 0 and t + 1 < PIECES:
+            send_own(t + 1)
+        if p + t > 1 and rotated < PIECES:
+            rotate(rotated)
+            rotated += 1
+        if t == long:
+            gathered(p)
+            if p < PIECES - 1:
+                multiply(p, slice(0, rows * LAGS))
 
     ext_all = w[PIECES - 1, :, :, depth:depth + EXT].reshape(n * rows, EXT)
     row = lax.broadcasted_iota(jnp.int32, (16, EXT), 0)
@@ -238,33 +248,44 @@
     flag_cols = jnp.where((lane >= 6) & (lane < 6 + SEG), ext, 0.0).astype(jnp.bfloat16)
     pairs = lax.dot_general(flag_cols, ext_all, nt, preferred_element_type=jnp.float32)
     denominator = 1.0 / (jnp.maximum(pairs, 1.0) * math.sqrt(FREQ))
-    weight = [own[g] * theirs[g:g + 1] * denominator for g in range(SEG)]
-
-    for q in range(nb):
-        cols = slice(q * share, (q + 1) * share)
-        for a in range(rows):
+    for g in range(SEG):
+        weight[g] = own[g] * theirs[g:g + 1] * denominator
+
+    def stack(q, first, last):
+        cols = pl.ds(pl.multiple_of(q * share, share), share)
+        left_factor, right_factor = weight[0, :, cols], weight[1, :, cols]
+        for a in range(first, last):
             lines = slice(a * LAGS, (a + 1) * LAGS)
             part[q, lines] = (
-                acc[0, lines, cols] * weight[0][a:a + 1, cols]
-                + acc[1, lines, cols] * weight[1][a:a + 1, cols]
+                acc[0, lines, cols] * left_factor[a:a + 1]
+                + acc[1, lines, cols] * right_factor[a:a + 1]
             )
+
     copies = []
-    for k in range(1, nb):
-        target = lax.rem(band + k, nb)
-        copies.append(pltpu.make_async_remote_copy(
-            src_ref=part.at[target], dst_ref=got.at[k],
-            send_sem=part_send.at[k], recv_sem=part_recv.at[k],
-            device_id={"band": target}, device_id_type=MESH,
-        ))
-        copies[-1].start()
+    for m in range(2):
+        first, last = m * rows // 2, (m + 1) * rows // 2
+        lines = slice(first * LAGS, last * LAGS)
+        multiply(PIECES - 1, lines)
+        for k in range(1, nb):
+            target = lax.rem(band + k, nb)
+            stack(target, first, last)
+            copies.append(pltpu.make_async_remote_copy(
+                src_ref=part.at[target, lines], dst_ref=got.at[k, lines],
+                send_sem=part_send.at[k, m], recv_sem=part_recv.at[k, m],
+                device_id={"band": target}, device_id_type=MESH,
+            ))
+            copies[-1].start()
+    stack(band, 0, rows)
     for copy in sent + en_copies:
         copy.wait_send()
-    for copy in copies:
-        copy.wait()
-    result = part[band]
-    for k in range(1, nb):
-        result = result + got[k]
-    out_ref[...] = result
+    for m in range(2):
+        lines = slice(m * rows // 2 * LAGS, (m + 1) * rows // 2 * LAGS)
+        for copy in copies[m * (nb - 1):(m + 1) * (nb - 1)]:
+            copy.wait()
+        result = part[band, lines]
+        for k in range(1, nb):
+            result = result + got[k, lines]
+        out_ref[lines] = result
 
 
 def solution(mesh):
@@ -289,11 +310,12 @@
                 pltpu.VMEM((LAGS, freq), jnp.float32),
                 pltpu.VMEM((SEG, rows * LAGS, n * rows), jnp.float32),
                 pltpu.VMEM((nb, rows, EXT), jnp.float32),
+                pltpu.VMEM((SEG, rows, n * rows), jnp.float32),
                 pltpu.VMEM((nb, rows * LAGS, share), jnp.float32),
                 pltpu.VMEM((nb, rows * LAGS, share), jnp.float32),
                 dma((2, PIECES, chips)), dma((2, PIECES, chips)),
                 dma((PIECES, chips)), dma((PIECES, chips)),
-                dma((nb,)), dma((nb,)), dma((nb,)), dma((nb,)),
+                dma((nb,)), dma((nb,)), dma((nb, 2)), dma((nb, 2)),
             ],
             compiler_params=pltpu.CompilerParams(
                 collective_id=0, has_side_effects=True, vmem_limit_bytes=48 * 1024 * 1024

time: 46 us -> 45.8 us (level)
  no operation moved by 1% of the time
where the time goes in v2:
time: 45.8 us; the launch traced here: 45.6 us
  Pallas kernels  42.9 us (94%)
  local copies, waits for them, and re-layouts  2.69 us (6%)
    pallas_call x1, Pallas kernels, local(): pl.pallas_call(functools.partial(kernel, n, nb), out_shape=jax.ShapeDtype...  42.9 us
    unnamed x5, local copies, waits for them, and re-layouts  1.56 us
    reshape x1, local copies, waits for them, and re-layouts, local(): spectra.reshape(rows, SEG * 2 * freq)  1.13 us

profile of v2, /device:TPU:0, one launch (start us, length us, event | category | flops | bytes accessed | tf_op | source)
XLA Modules:
  0.0 45.6 jit_solution(16110192032380797200)
XLA Ops:
  0.0 0.0 copy-start
  0.0 0.8 %copy.4.flags_ref = s32[16,2]{1,0:T(8,128)S(1)} copy(s32[16,2]{0,1:T(2,128)} %param.4) | data formatting | bytes 256 | tf_op args[1]
  0.8 0.0 copy-done
  0.8 0.1 copy.5.band_ref
  0.9 1.1 %reshape.6.x_ref = bf16[16,8192]{1,0:T(8,128)(2,1)S(1)} reshape(bf16[16,2,2,2048]{3,2,1,0:T(2,128)(2,1)} %param.3) | data formatting | bytes 524288 | tf_op jit(solution)/shard_map/reshape | solution.py:323
  2.0 42.9 %shard_map.37 = f32[512,128]{1,0:T(8,128)S(1)} custom-call(bf16[16,8192]{1,0:T(8,128)(2,1)S(1)} %reshape.6.x_ref, s32[16,2]{1,0:T(8,128)S(1)} %copy.4.flags_ref, s32[16,2]{1,0:T(8,128)S(1)} %copy.5.band_ref), custom_call_target="tpu_custom_call" | custom-call | tf_op jit(solution)/shard_map/pallas_call | solution.py:301
  44.9 0.7 %copy.7 = f32[16,32,128]{2,1,0:T(8,128)} copy(f32[16,32,128]{2,1,0:T(8,128)S(1)} %bitcast.1) | data formatting | bytes 524288
Async XLA Ops:
  0.0 0.8 %copy-start = (s32[16,2]{0,1:T(2,128)S(1)}, s32[16,2]{0,1:T(2,128)}, u32[]{:S(2)}) copy-start(s32[16,2]{0,1:T(2,128)} %param.5) | copy-start | bytes 388

commit v3 on v2

--- a/solution.py
+++ b/solution.py
@@ -129,6 +129,7 @@
 
     send_own(0)
     send_own(1)
+    send_own(2)
 
     for k in range(1, nb):
         source = lax.rem(band + nb - k, nb)
@@ -155,8 +156,7 @@
         ext = jnp.where(lane == 6 + g, valid, ext)
     w[PIECES - 1, me, :, depth:depth + EXT] = ext.astype(jnp.bfloat16)
 
-    @pl.loop(0, freq // 128)
-    def _(j):
+    def phases(j):
         cols = pl.ds(pl.multiple_of(j * 128, 128), 128)
         lag = lax.broadcasted_iota(jnp.int32, (LAGS, 128), 0) - LAGS // 2
         f = band * freq + j * 128 + lax.broadcasted_iota(jnp.int32, (LAGS, 128), 1)
@@ -165,10 +165,10 @@
         cos_ref[:, cols] = jnp.cos(phase)
         sin_ref[:, cols] = jnp.sin(phase)
 
-    def rotate(p):
+    def rotate(p, first, last):
         h = p % 2
 
-        @pl.loop(0, half // 128)
+        @pl.loop(first, last)
         def _(j):
             at = pl.multiple_of(j * 128, 128)
             table = pl.ds(pl.multiple_of(h * half + j * 128, 128), 128)
@@ -224,18 +224,24 @@
         ((p, t) for p in range(PIECES) for t in range(1, long + 1)),
         key=lambda pt: (pt[0] + pt[1], -pt[0]),
     )
-    rotated = 0
-    for p, t in order:
+    blocks = half // 128
+    work = [functools.partial(pl.loop(blocks, 2 * blocks), phases)]
+    for p in range(PIECES):
+        work.append(functools.partial(rotate, p, 0, blocks // 2))
+        work.append(functools.partial(rotate, p, blocks // 2, blocks))
+    pl.loop(0, blocks)(phases)
+    done = 0
+    for index, (p, t) in enumerate(order):
         hop(p, t)
-        if p == 0 and t + 1 < PIECES:
-            send_own(t + 1)
-        if p + t > 1 and rotated < PIECES:
-            rotate(rotated)
-            rotated += 1
-        if t == long:
-            gathered(p)
-            if p < PIECES - 1:
-                multiply(p, slice(0, rows * LAGS))
+        if (p, t) == (0, 1):
+            send_own(PIECES - 1)
+        if work:
+            work.pop(0)()
+        if len(order) - index <= PIECES - 1:
+            gathered(done)
+            multiply(done, slice(0, rows * LAGS))
+            done += 1
+    gathered(PIECES - 1)
 
     ext_all = w[PIECES - 1, :, :, depth:depth + EXT].reshape(n * rows, EXT)
     row = lax.broadcasted_iota(jnp.int32, (16, EXT), 0)

time: 45.8 us -> 43.6 us (0.952)
  Pallas kernels: 42.9 us -> 40.7 us
    pallas_call x1, Pallas kernels: 42.9 us -> 40.7 us  [local(): pl.pallas_call(functools.partial(kernel, n, nb), out_shape=jax.ShapeDtype...]
where the time goes in v3:
time: 43.6 us; the launch traced here: 43.4 us
  Pallas kernels  40.7 us (93%)
  local copies, waits for them, and re-layouts  2.69 us (6%)
    pallas_call x1, Pallas kernels, local(): pl.pallas_call(functools.partial(kernel, n, nb), out_shape=jax.ShapeDtype...  40.7 us
    unnamed x5, local copies, waits for them, and re-layouts  1.56 us
    reshape x1, local copies, waits for them, and re-layouts, local(): spectra.reshape(rows, SEG * 2 * freq)  1.13 us

profile of v3, /device:TPU:0, one launch (start us, length us, event | category | flops | bytes accessed | tf_op | source)
XLA Modules:
  0.0 43.4 jit_solution(5812823111832735291)
XLA Ops:
  0.0 0.0 copy-start
  0.0 0.8 %copy.4.flags_ref = s32[16,2]{1,0:T(8,128)S(1)} copy(s32[16,2]{0,1:T(2,128)} %param.4) | data formatting | bytes 256 | tf_op args[1]
  0.8 0.0 copy-done
  0.8 0.1 copy.5.band_ref
  0.9 1.1 %reshape.6.x_ref = bf16[16,8192]{1,0:T(8,128)(2,1)S(1)} reshape(bf16[16,2,2,2048]{3,2,1,0:T(2,128)(2,1)} %param.3) | data formatting | bytes 524288 | tf_op jit(solution)/shard_map/reshape | solution.py:329
  2.0 40.7 %shard_map.37 = f32[512,128]{1,0:T(8,128)S(1)} custom-call(bf16[16,8192]{1,0:T(8,128)(2,1)S(1)} %reshape.6.x_ref, s32[16,2]{1,0:T(8,128)S(1)} %copy.4.flags_ref, s32[16,2]{1,0:T(8,128)S(1)} %copy.5.band_ref), custom_call_target="tpu_custom_call" | custom-call | tf_op jit(solution)/shard_map/pallas_call | solution.py:307
  42.7 0.7 %copy.7 = f32[16,32,128]{2,1,0:T(8,128)} copy(f32[16,32,128]{2,1,0:T(8,128)S(1)} %bitcast.1) | data formatting | bytes 524288
Async XLA Ops:
  0.0 0.8 %copy-start = (s32[16,2]{0,1:T(2,128)S(1)}, s32[16,2]{0,1:T(2,128)}, u32[]{:S(2)}) copy-start(s32[16,2]{0,1:T(2,128)} %param.5) | copy-start | bytes 388

commit v4 on v3

--- a/solution.py
+++ b/solution.py
@@ -220,10 +220,14 @@
             else:
                 acc[g, lines] += term
 
-    order = sorted(
-        ((p, t) for p in range(PIECES) for t in range(1, long + 1)),
-        key=lambda pt: (pt[0] + pt[1], -pt[0]),
-    )
+    waiting, order = [(p, 1) for p in range(PIECES - 1)], []
+    while waiting:
+        p, t = waiting.pop(0)
+        order.append((p, t))
+        if t < long:
+            waiting.append((p, t + 1))
+        if (p, t) == (0, 1):
+            waiting.append((PIECES - 1, 1))
     blocks = half // 128
     work = [functools.partial(pl.loop(blocks, 2 * blocks), phases)]
     for p in range(PIECES):

time: 43.6 us -> 43.1 us (0.989)
    pallas_call x1, Pallas kernels: 40.7 us -> 40.3 us  [local(): pl.pallas_call(functools.partial(kernel, n, nb), out_shape=jax.ShapeDtype...]
where the time goes in v4:
time: 43.1 us; the launch traced here: 43 us
  Pallas kernels  40.3 us (94%)
  local copies, waits for them, and re-layouts  2.69 us (6%)
    pallas_call x1, Pallas kernels, local(): pl.pallas_call(functools.partial(kernel, n, nb), out_shape=jax.ShapeDtype...  40.3 us
    unnamed x5, local copies, waits for them, and re-layouts  1.56 us
    reshape x1, local copies, waits for them, and re-layouts, local(): spectra.reshape(rows, SEG * 2 * freq)  1.13 us

profile of v4, /device:TPU:0, one launch (start us, length us, event | category | flops | bytes accessed | tf_op | source)
XLA Modules:
  0.0 43.0 jit_solution(652852951331263619)
XLA Ops:
  0.0 0.0 copy-start
  0.0 0.8 %copy.4.flags_ref = s32[16,2]{1,0:T(8,128)S(1)} copy(s32[16,2]{0,1:T(2,128)} %param.4) | data formatting | bytes 256 | tf_op args[1]
  0.8 0.0 copy-done
  0.8 0.1 copy.5.band_ref
  0.9 1.1 %reshape.6.x_ref = bf16[16,8192]{1,0:T(8,128)(2,1)S(1)} reshape(bf16[16,2,2,2048]{3,2,1,0:T(2,128)(2,1)} %param.3) | data formatting | bytes 524288 | tf_op jit(solution)/shard_map/reshape | solution.py:333
  2.0 40.3 %shard_map.37 = f32[512,128]{1,0:T(8,128)S(1)} custom-call(bf16[16,8192]{1,0:T(8,128)(2,1)S(1)} %reshape.6.x_ref, s32[16,2]{1,0:T(8,128)S(1)} %copy.4.flags_ref, s32[16,2]{1,0:T(8,128)S(1)} %copy.5.band_ref), custom_call_target="tpu_custom_call" | custom-call | tf_op jit(solution)/shard_map/pallas_call | solution.py:311
  42.3 0.7 %copy.7 = f32[16,32,128]{2,1,0:T(8,128)} copy(f32[16,32,128]{2,1,0:T(8,128)S(1)} %bitcast.1) | data formatting | bytes 524288
Async XLA Ops:
  0.0 0.8 %copy-start = (s32[16,2]{0,1:T(2,128)S(1)}, s32[16,2]{0,1:T(2,128)}, u32[]{:S(2)}) copy-start(s32[16,2]{0,1:T(2,128)} %param.5) | copy-start | bytes 388
